TPU v7x, 32 devices: a whole 2x2x4 slice. The times are simulated.
32 devices in a mesh: date: 4 (over y, x), az: 8 (over z, core).
Axes of the slice: x: 2, y: 2, z: 4, core: 2. Of those that a mesh axis runs over, the one named last changes fastest.
Arguments:
- epoch_image_tensor: bfloat16 [16, 2, 2560, 1280], P('date', None, 'az'), may hold values from -5 to 5
- along_track_shifts: int32 [16, 40, 20], P('date', 'az'), may hold values from -32 to 32, as said below
- cross_track_shifts: int32 [16, 40, 20], P('date', 'az'), may hold values from -32 to 32, as said below
- epoch_present_table: int32 [16, 40], P('date', 'az'), may hold values 0 or 1
Outputs:
- tile_similarity: float32 [16, 40, 20], P('date', 'az')
- smoothed_ifgs: float32 [16, 2, 512, 64], P('date', None, 'az')
Inputs may be any that keep to these rules, and one draw needn't show every extreme that they name: `along_track_shifts`: date 0 has all offsets zero. `cross_track_shifts`: date 0 has all offsets zero.
All inputs are finite; a program needn't handle non-finite values. Where the computation divides by a largest or mean magnitude, that divisor is 1e-20 or more. No bound on the sum of `epoch_present_table` on one device may be relied on, other than what follows from the above.
Results may differ from a plain program's by a relative error of at most 0.0003.
Values may be sent and summed in bfloat16 or wider, within the bound.
A program may use at most 192 MiB of HBM per device.

v0:
```python
import math

import jax
import jax.numpy as jnp
from jax import lax
from jax.sharding import PartitionSpec as P

WIN = 64
MARGIN_LINES = 32
RHALO = 32
LOOK_AZ = 5
LOOK_RG = 20
PATCH = 32


VAR_EPS = 1e-05
RMS_EPS = 1e-06


def broadcast(x, axis, root):
    mine = lax.axis_index(axis) == root
    return lax.psum(jnp.where(mine, x, jnp.zeros_like(x)), axis)


def extended(block, sides, width):
    for axis, dim in sides:
        count = lax.axis_size(axis)
        forward = [(i, i + 1) for i in range(count - 1)]
        backward = [(target, source) for source, target in forward]
        low = lax.ppermute(
            lax.slice_in_dim(block, block.shape[dim] - width, None, axis=dim), axis, forward
        )
        high = lax.ppermute(lax.slice_in_dim(block, 0, width, axis=dim), axis, backward)
        block = jnp.concatenate([low, block, high], axis=dim)
    return block


def goldstein_filter(looks):
    epochs_present = looks.shape[0]
    present_lines = looks.shape[2]
    samples_here = looks.shape[3]
    highest = lax.Precision.HIGHEST
    positions = jnp.arange(PATCH, dtype=jnp.int32)
    turns = positions[:, None] * positions[None, :] % PATCH
    angles = turns.astype(jnp.float32) * (2.0 * math.pi / PATCH)
    cosine = jnp.cos(angles)
    sine = jnp.sin(angles)
    shape_five = (epochs_present, present_lines // PATCH, PATCH, samples_here // PATCH, PATCH)
    real_part = looks[:, 0].reshape(shape_five)
    imag_part = looks[:, 1].reshape(shape_five)

    def along_rows(table, values):
        return jnp.einsum("ki,daibj->dakbj", table, values, precision=highest)

    def along_cols(table, values):
        return jnp.einsum("lj,dakbj->dakbl", table, values, precision=highest)

    first_real = along_rows(cosine, real_part) + along_rows(sine, imag_part)
    first_imag = along_rows(cosine, imag_part) - along_rows(sine, real_part)
    spec_real = along_cols(cosine, first_real) + along_cols(sine, first_imag)
    spec_imag = along_cols(cosine, first_imag) - along_cols(sine, first_real)
    magnitude = jnp.sqrt(spec_real**2 + spec_imag**2)
    smooth = jnp.zeros_like(magnitude)
    for shift_a in (-1, 0, 1):
        for shift_b in (-1, 0, 1):
            smooth = smooth + jnp.roll(magnitude, (shift_a, shift_b), axis=(2, 4))
    weight = jnp.sqrt(smooth / 9.0)
    weighted_real = spec_real * weight
    weighted_imag = spec_imag * weight
    back_real = along_rows(cosine, weighted_real) - along_rows(sine, weighted_imag)
    back_imag = along_rows(cosine, weighted_imag) + along_rows(sine, weighted_real)
    out_real = along_cols(cosine, back_real) - along_cols(sine, back_imag)
    out_imag = along_cols(cosine, back_imag) + along_cols(sine, back_real)
    power = jnp.mean(out_real**2 + out_imag**2, axis=(2, 4), keepdims=True)
    scaling = 1.0 / jnp.sqrt(power + RMS_EPS)
    result = jnp.stack([out_real * scaling, out_imag * scaling], axis=1)
    return result.reshape(epochs_present, 2, present_lines, samples_here)


def on_device(epoch_image_tensor, along_track_shifts, cross_track_shifts, epoch_present_table):
    epochs_present = epoch_image_tensor.shape[0]
    present_lines = epoch_image_tensor.shape[2]
    pixel_values = epoch_image_tensor.shape[3]
    windows_az = present_lines // WIN
    windows_rg = pixel_values // WIN
    span_count = 1 + 2 * RHALO // WIN
    primary_strip = epoch_image_tensor[0]
    shared_band = broadcast(primary_strip, "date", 0)

    def process(padded, tile_line_number, carry):
        corr_buffer, moved_buffer, ref_buffer = carry
        ref_rows = lax.dynamic_slice_in_dim(shared_band, tile_line_number * WIN, WIN, 1)
        strip = lax.dynamic_slice_in_dim(padded, tile_line_number * WIN, WIN + 2 * MARGIN_LINES, 2)
        blocks = strip.reshape(
            epochs_present, 2, WIN + 2 * MARGIN_LINES, padded.shape[3] // WIN, WIN
        )
        slabs = jnp.concatenate(
            [blocks[:, :, :, offset : offset + windows_rg, :] for offset in range(span_count)],
            axis=4,
        )
        shift_rows = lax.dynamic_index_in_dim(
            along_track_shifts, tile_line_number, 1, keepdims=False
        )
        shift_cols = lax.dynamic_index_in_dim(
            cross_track_shifts, tile_line_number, 1, keepdims=False
        )
        nearby = jnp.arange(WIN, dtype=jnp.int32)
        pick_rows = (
            jnp.arange(WIN + 2 * MARGIN_LINES, dtype=jnp.int32)[None, None, None, :]
            == nearby[None, None, :, None] + MARGIN_LINES + shift_rows[:, :, None, None]
        ).astype(jnp.bfloat16)
        pick_cols = (
            jnp.arange(WIN + 2 * RHALO, dtype=jnp.int32)[None, None, :, None]
            == nearby[None, None, None, :] + RHALO + shift_cols[:, :, None, None]
        ).astype(jnp.bfloat16)
        shifted = jnp.einsum(
            "dwia,dcawb->dcwib", pick_rows, slabs, preferred_element_type=jnp.float32
        ).astype(jnp.bfloat16)
        moved = jnp.einsum(
            "dcwib,dwbj->dciwj", shifted, pick_cols, preferred_element_type=jnp.float32
        )
        keep_flag = lax.dynamic_index_in_dim(
            epoch_present_table, tile_line_number, 1, keepdims=False
        )
        moved = moved * keep_flag.astype(jnp.float32)[:, None, None, None, None]
        lead_rows = ref_rows.astype(jnp.float32).reshape(2, WIN, windows_rg, WIN)
        ref_amp = jnp.sqrt(lead_rows[0] ** 2 + lead_rows[1] ** 2)
        ref_dev = ref_amp - jnp.mean(ref_amp, axis=(0, 2), keepdims=True)
        ref_var = jnp.mean(ref_dev**2, axis=(0, 2))
        sec_amp = jnp.sqrt(moved[:, 0] ** 2 + moved[:, 1] ** 2)
        sec_dev = sec_amp - jnp.mean(sec_amp, axis=(1, 3), keepdims=True)
        sec_var = jnp.mean(sec_dev**2, axis=(1, 3))
        covariance = jnp.mean(ref_dev[None] * sec_dev, axis=(1, 3))
        corr = covariance / jnp.sqrt((ref_var[None, :] + VAR_EPS) * (sec_var + VAR_EPS))
        moved_rows = moved.astype(jnp.bfloat16).reshape(epochs_present, 2, WIN, pixel_values)
        corr_buffer = lax.dynamic_update_slice_in_dim(
            corr_buffer, corr[:, None, :], tile_line_number, 1
        )
        moved_buffer = lax.dynamic_update_slice_in_dim(
            moved_buffer, moved_rows, tile_line_number * WIN, 2
        )
        ref_buffer = lax.dynamic_update_slice_in_dim(
            ref_buffer, ref_rows, tile_line_number * WIN, 1
        )
        return (corr_buffer, moved_buffer, ref_buffer)

    initial = (
        jnp.zeros((epochs_present, windows_az, windows_rg), jnp.float32),
        jnp.zeros((epochs_present, 2, present_lines, pixel_values), jnp.bfloat16),
        jnp.zeros((2, present_lines, pixel_values), jnp.bfloat16),
    )
    cross_track_margin = ((0, 0), (0, 0), (0, 0), (RHALO, RHALO))
    widened_image = jnp.pad(
        extended(epoch_image_tensor, (("az", 2),), MARGIN_LINES), cross_track_margin
    )
    carry = lax.fori_loop(
        0,
        windows_az,
        lambda tile_line_number, state: process(widened_image, tile_line_number, state),
        initial,
    )
    corr_buffer, moved_buffer, ref_buffer = carry
    lead_band = ref_buffer.astype(jnp.float32)
    moved_band = moved_buffer.astype(jnp.float32)
    ifg_real = lead_band[0][None] * moved_band[:, 0] + lead_band[1][None] * moved_band[:, 1]
    ifg_imag = lead_band[1][None] * moved_band[:, 0] - lead_band[0][None] * moved_band[:, 1]
    ifg_band = jnp.stack([ifg_real, ifg_imag], axis=1)
    range_pool = (
        jnp.arange(pixel_values, dtype=jnp.int32)[:, None] // LOOK_RG
        == jnp.arange(pixel_values // LOOK_RG, dtype=jnp.int32)[None, :]
    ).astype(jnp.float32)
    azimuth_pool = (
        jnp.arange(present_lines // LOOK_AZ, dtype=jnp.int32)[:, None]
        == jnp.arange(present_lines, dtype=jnp.int32)[None, :] // LOOK_AZ
    ).astype(jnp.float32)
    range_looks = jnp.einsum("dcar,rm->dcam", ifg_band, range_pool, precision=lax.Precision.HIGHEST)
    looks = jnp.einsum("la,dcam->dclm", azimuth_pool, range_looks, precision=lax.Precision.HIGHEST)
    return (corr_buffer, goldstein_filter(looks))


def solution(mesh):
    placed = (
        P("date", None, "az", None),
        P("date", "az", None),
        P("date", "az", None),
        P("date", "az"),
    )
    return jax.shard_map(
        on_device,
        mesh=mesh,
        in_specs=placed,
        out_specs=(P("date", "az", None), P("date", None, "az", None)),
        check_vma=False,
    )
```

profile of v0, /device:TPU:28, one launch (start us, length us, event | category | flops | bytes accessed | tf_op | source)
XLA Modules:
  0.0 420.6 jit_solution(17419590410467638537)
XLA Ops:
  10.6 3.6 collective-permute-start.1
  14.2 9.9 %copy.85 = bf16[4,2,320,1280]{2,3,1,0:T(8,128)(2,1)} copy(bf16[4,2,320,1280]{3,2,1,0:T(8,128)(2,1)} %param.6) | data formatting | bytes 13107200 | tf_op args[0]
  30.2 3.5 copy.88
  33.7 10.4 %fusion.47 = bf16[4,2,384,1344]{2,3,1,0:T(8,128)(2,1)} fusion(bf16[4,2,32,1280]{2,3,1,0:T(8,128)(2,1)} %copy.88, bf16[4,2,320,1280]{2,3,1,0:T(8,128)(2,1)} %copy.85, bf16[4,2,32,1280]{2,3,1,0:T(8,128)(2,1)S(1)} %copy.86), kind=kLoop, calls=%fused_computation.58 | loop fusion | flops 49545216 | bytes 16121856 | tf_op jit(solution)/shard_map/concatenate | solution.py:34
  44.2 51.4 %all-reduce.3.cloned.1.call-done = bf16[2,320,1280]{1,2,0:T(8,128)(2,1)} async-done(((bf16[2,320,1280]{1,2,0:T(8,128)(2,1)}), bf16[2,320,1280]{1,2,0:T(8,128)(2,1)}) %all-reduce.3.cloned.1.call-update) | async-done | bytes 1638416 | tf_op jit(solution)/shard_map/psum | solution.py:22
  100.2 275.7 %while.17 = (s32[]{:T(128)}, f32[4,5,20]{2,0,1:T(4,128)S(1)}, bf16[4,2,320,1280]{3,2,1,0:T(8,128)(2,1)}, bf16[2,320,1280]{1,2,0:T(8,128)(2,1)}, bf16[2,320,1280]...) while((s32[]{:T(128)}, f32[4,5,20]{2,0,1:T(4,128)S(1)}, ...), condition=%wide.region_9.10_spmd, body=%wide.region_1.9_spmd.sunk | while | flops 522496320 | bytes 53173928 | solution.py:156
  100.2 3.5 constant_dynamic-slice_fusion.5
  106.5 6.0 %copy.142 = bf16[4,2,128,20,64]{4,2,1,3,0:T(8,128)(2,1)} copy(bf16[4,2,128,20,64]{2,4,3,1,0:T(8,128)(2,1)} %get-tuple-element.338) | data formatting | bytes 5242880 | tf_op jit(solution)/shard_map/while
  112.5 4.1 copy.143
  117.4 10.3 %fusion.241 = (bf16[4,2,64,20,64]{2,4,1,3,0:T(8,128)(2,1)}, f32[4,2,64,20,64]{2,4,1,3,0:T(8,128)}) fusion(f32[4]{0:T(128)S(1)} %fusion.239, bf16[4,2,128,20,64]{4,2,1,3,0:T(8,128)(2,1)} %copy.142, bf16[4,2,128,20,64]{4,2,1,3,0:T(8,128)(2,1)} %copy.143, s32[4,20,64]{2,1,0:T(8,128)S(1)} %get-tuple-element.342, s32[4,20,64]{2,1,0:T(8,128)S(1)} %get-tuple-element.343), kind=kOutput, calls=%fused_computation.243.clone.1 | convolution fusion | flops 517734400 | bytes 9216016 | tf_op jit(solution)/shard_map/while/body/eval_jaxpr/dcwib,dwbj->dciwj/dot_general | solution.py:119
  127.7 3.5 copy.144
  136.5 3.7 fusion.242
  142.2 4.3 %multiply_reduce_fusion.5 = (f32[4,20]{1,0:T(4,128)S(1)}, f32[4,20]{1,0:T(4,128)S(1)}) fusion(f32[4,20]{1,0:T(4,128)S(1)} %broadcast_multiply_fusion.6, f32[64,20,64]{0,2,1:T(8,128)S(1)} %broadcast_subtract_fusion.2, f32[4,2,64,20,64]{2,4,1,3,0:T(8,128)} %get-tuple-element.344), kind=kLoop, calls=%fused_computation.13.clone.1 | loop fusion | flops 2621280 | bytes 2950080 | tf_op jit(solution)/shard_map/while/body/eval_jaxpr/reduce_sum | solution.py:133
  147.3 7.9 %dynamic_update_slice.28 = bf16[2,320,1280]{1,2,0:T(8,128)(2,1)} dynamic-update-slice(bf16[2,320,1280]{1,2,0:T(8,128)(2,1)} %get-tuple-element.370, bf16[2,64,1280]{1,2,0:T(8,128)(2,1)S(1)} %get-tuple-element.351, s32[]{:T(128)} %constant.135.clone.1..sunk, s32[]{:T(128)S(6)} %select_n.170, s32[]{:T(128)} %constant.135.clone.1..sunk) | dynamic-update-slice | bytes 655364 | tf_op jit(solution)/shard_map/while/body/eval_jaxpr/dynamic_update_slice | solution.py:142
  155.2 3.5 constant_dynamic-slice_fusion.5
  161.6 6.0 %copy.142 = bf16[4,2,128,20,64]{4,2,1,3,0:T(8,128)(2,1)} copy(bf16[4,2,128,20,64]{2,4,3,1,0:T(8,128)(2,1)} %get-tuple-element.338) | data formatting | bytes 5242880 | tf_op jit(solution)/shard_map/while
  167.5 4.1 copy.143
  172.5 10.3 %fusion.241 = (bf16[4,2,64,20,64]{2,4,1,3,0:T(8,128)(2,1)}, f32[4,2,64,20,64]{2,4,1,3,0:T(8,128)}) fusion(f32[4]{0:T(128)S(1)} %fusion.239, bf16[4,2,128,20,64]{4,2,1,3,0:T(8,128)(2,1)} %copy.142, bf16[4,2,128,20,64]{4,2,1,3,0:T(8,128)(2,1)} %copy.143, s32[4,20,64]{2,1,0:T(8,128)S(1)} %get-tuple-element.342, s32[4,20,64]{2,1,0:T(8,128)S(1)} %get-tuple-element.343), kind=kOutput, calls=%fused_computation.243.clone.1 | convolution fusion | flops 517734400 | bytes 9216016 | tf_op jit(solution)/shard_map/while/body/eval_jaxpr/dcwib,dwbj->dciwj/dot_general | solution.py:119
  182.8 3.5 copy.144
  191.5 3.7 fusion.242
  197.2 4.3 %multiply_reduce_fusion.5 = (f32[4,20]{1,0:T(4,128)S(1)}, f32[4,20]{1,0:T(4,128)S(1)}) fusion(f32[4,20]{1,0:T(4,128)S(1)} %broadcast_multiply_fusion.6, f32[64,20,64]{0,2,1:T(8,128)S(1)} %broadcast_subtract_fusion.2, f32[4,2,64,20,64]{2,4,1,3,0:T(8,128)} %get-tuple-element.344), kind=kLoop, calls=%fused_computation.13.clone.1 | loop fusion | flops 2621280 | bytes 2950080 | tf_op jit(solution)/shard_map/while/body/eval_jaxpr/reduce_sum | solution.py:133
  202.3 9.0 %dynamic_update_slice.28 = bf16[2,320,1280]{1,2,0:T(8,128)(2,1)} dynamic-update-slice(bf16[2,320,1280]{1,2,0:T(8,128)(2,1)} %get-tuple-element.370, bf16[2,64,1280]{1,2,0:T(8,128)(2,1)S(1)} %get-tuple-element.351, s32[]{:T(128)} %constant.135.clone.1..sunk, s32[]{:T(128)S(6)} %select_n.170, s32[]{:T(128)} %constant.135.clone.1..sunk) | dynamic-update-slice | bytes 655364 | tf_op jit(solution)/shard_map/while/body/eval_jaxpr/dynamic_update_slice | solution.py:142
  211.3 3.5 constant_dynamic-slice_fusion.5
  217.7 6.0 %copy.142 = bf16[4,2,128,20,64]{4,2,1,3,0:T(8,128)(2,1)} copy(bf16[4,2,128,20,64]{2,4,3,1,0:T(8,128)(2,1)} %get-tuple-element.338) | data formatting | bytes 5242880 | tf_op jit(solution)/shard_map/while
  223.6 4.1 copy.143
  228.6 10.3 %fusion.241 = (bf16[4,2,64,20,64]{2,4,1,3,0:T(8,128)(2,1)}, f32[4,2,64,20,64]{2,4,1,3,0:T(8,128)}) fusion(f32[4]{0:T(128)S(1)} %fusion.239, bf16[4,2,128,20,64]{4,2,1,3,0:T(8,128)(2,1)} %copy.142, bf16[4,2,128,20,64]{4,2,1,3,0:T(8,128)(2,1)} %copy.143, s32[4,20,64]{2,1,0:T(8,128)S(1)} %get-tuple-element.342, s32[4,20,64]{2,1,0:T(8,128)S(1)} %get-tuple-element.343), kind=kOutput, calls=%fused_computation.243.clone.1 | convolution fusion | flops 517734400 | bytes 9216016 | tf_op jit(solution)/shard_map/while/body/eval_jaxpr/dcwib,dwbj->dciwj/dot_general | solution.py:119
  238.9 3.5 copy.144
  247.6 3.7 fusion.242
  253.4 4.3 %multiply_reduce_fusion.5 = (f32[4,20]{1,0:T(4,128)S(1)}, f32[4,20]{1,0:T(4,128)S(1)}) fusion(f32[4,20]{1,0:T(4,128)S(1)} %broadcast_multiply_fusion.6, f32[64,20,64]{0,2,1:T(8,128)S(1)} %broadcast_subtract_fusion.2, f32[4,2,64,20,64]{2,4,1,3,0:T(8,128)} %get-tuple-element.344), kind=kLoop, calls=%fused_computation.13.clone.1 | loop fusion | flops 2621280 | bytes 2950080 | tf_op jit(solution)/shard_map/while/body/eval_jaxpr/reduce_sum | solution.py:133
  258.5 7.9 %dynamic_update_slice.28 = bf16[2,320,1280]{1,2,0:T(8,128)(2,1)} dynamic-update-slice(bf16[2,320,1280]{1,2,0:T(8,128)(2,1)} %get-tuple-element.370, bf16[2,64,1280]{1,2,0:T(8,128)(2,1)S(1)} %get-tuple-element.351, s32[]{:T(128)} %constant.135.clone.1..sunk, s32[]{:T(128)S(6)} %select_n.170, s32[]{:T(128)} %constant.135.clone.1..sunk) | dynamic-update-slice | bytes 655364 | tf_op jit(solution)/shard_map/while/body/eval_jaxpr/dynamic_update_slice | solution.py:142
  266.3 3.5 constant_dynamic-slice_fusion.5
  272.7 6.0 %copy.142 = bf16[4,2,128,20,64]{4,2,1,3,0:T(8,128)(2,1)} copy(bf16[4,2,128,20,64]{2,4,3,1,0:T(8,128)(2,1)} %get-tuple-element.338) | data formatting | bytes 5242880 | tf_op jit(solution)/shard_map/while
  278.6 4.1 copy.143
  283.6 10.3 %fusion.241 = (bf16[4,2,64,20,64]{2,4,1,3,0:T(8,128)(2,1)}, f32[4,2,64,20,64]{2,4,1,3,0:T(8,128)}) fusion(f32[4]{0:T(128)S(1)} %fusion.239, bf16[4,2,128,20,64]{4,2,1,3,0:T(8,128)(2,1)} %copy.142, bf16[4,2,128,20,64]{4,2,1,3,0:T(8,128)(2,1)} %copy.143, s32[4,20,64]{2,1,0:T(8,128)S(1)} %get-tuple-element.342, s32[4,20,64]{2,1,0:T(8,128)S(1)} %get-tuple-element.343), kind=kOutput, calls=%fused_computation.243.clone.1 | convolution fusion | flops 517734400 | bytes 9216016 | tf_op jit(solution)/shard_map/while/body/eval_jaxpr/dcwib,dwbj->dciwj/dot_general | solution.py:119
  293.9 3.5 copy.144
  302.6 3.7 fusion.242
  308.4 4.3 %multiply_reduce_fusion.5 = (f32[4,20]{1,0:T(4,128)S(1)}, f32[4,20]{1,0:T(4,128)S(1)}) fusion(f32[4,20]{1,0:T(4,128)S(1)} %broadcast_multiply_fusion.6, f32[64,20,64]{0,2,1:T(8,128)S(1)} %broadcast_subtract_fusion.2, f32[4,2,64,20,64]{2,4,1,3,0:T(8,128)} %get-tuple-element.344), kind=kLoop, calls=%fused_computation.13.clone.1 | loop fusion | flops 2621280 | bytes 2950080 | tf_op jit(solution)/shard_map/while/body/eval_jaxpr/reduce_sum | solution.py:133
  313.4 9.0 %dynamic_update_slice.28 = bf16[2,320,1280]{1,2,0:T(8,128)(2,1)} dynamic-update-slice(bf16[2,320,1280]{1,2,0:T(8,128)(2,1)} %get-tuple-element.370, bf16[2,64,1280]{1,2,0:T(8,128)(2,1)S(1)} %get-tuple-element.351, s32[]{:T(128)} %constant.135.clone.1..sunk, s32[]{:T(128)S(6)} %select_n.170, s32[]{:T(128)} %constant.135.clone.1..sunk) | dynamic-update-slice | bytes 655364 | tf_op jit(solution)/shard_map/while/body/eval_jaxpr/dynamic_update_slice | solution.py:142
  328.0 6.0 %copy.142 = bf16[4,2,128,20,64]{4,2,1,3,0:T(8,128)(2,1)} copy(bf16[4,2,128,20,64]{2,4,3,1,0:T(8,128)(2,1)} %get-tuple-element.338) | data formatting | bytes 5242880 | tf_op jit(solution)/shard_map/while
  333.9 4.1 copy.143
  338.9 10.3 %fusion.241 = (bf16[4,2,64,20,64]{2,4,1,3,0:T(8,128)(2,1)}, f32[4,2,64,20,64]{2,4,1,3,0:T(8,128)}) fusion(f32[4]{0:T(128)S(1)} %fusion.239, bf16[4,2,128,20,64]{4,2,1,3,0:T(8,128)(2,1)} %copy.142, bf16[4,2,128,20,64]{4,2,1,3,0:T(8,128)(2,1)} %copy.143, s32[4,20,64]{2,1,0:T(8,128)S(1)} %get-tuple-element.342, s32[4,20,64]{2,1,0:T(8,128)S(1)} %get-tuple-element.343), kind=kOutput, calls=%fused_computation.243.clone.1 | convolution fusion | flops 517734400 | bytes 9216016 | tf_op jit(solution)/shard_map/while/body/eval_jaxpr/dcwib,dwbj->dciwj/dot_general | solution.py:119
  349.2 3.5 copy.144
  358.0 3.7 fusion.242
  363.7 4.3 %multiply_reduce_fusion.5 = (f32[4,20]{1,0:T(4,128)S(1)}, f32[4,20]{1,0:T(4,128)S(1)}) fusion(f32[4,20]{1,0:T(4,128)S(1)} %broadcast_multiply_fusion.6, f32[64,20,64]{0,2,1:T(8,128)S(1)} %broadcast_subtract_fusion.2, f32[4,2,64,20,64]{2,4,1,3,0:T(8,128)} %get-tuple-element.344), kind=kLoop, calls=%fused_computation.13.clone.1 | loop fusion | flops 2621280 | bytes 2950080 | tf_op jit(solution)/shard_map/while/body/eval_jaxpr/reduce_sum | solution.py:133
  368.8 7.1 %dynamic_update_slice.28 = bf16[2,320,1280]{1,2,0:T(8,128)(2,1)} dynamic-update-slice(bf16[2,320,1280]{1,2,0:T(8,128)(2,1)} %get-tuple-element.370, bf16[2,64,1280]{1,2,0:T(8,128)(2,1)S(1)} %get-tuple-element.351, s32[]{:T(128)} %constant.135.clone.1..sunk, s32[]{:T(128)S(6)} %select_n.170, s32[]{:T(128)} %constant.135.clone.1..sunk) | dynamic-update-slice | bytes 655364 | tf_op jit(solution)/shard_map/while/body/eval_jaxpr/dynamic_update_slice | solution.py:142
  383.7 4.2 convert_element_type.88
  387.9 3.7 multiply_add_fusion.1
  391.6 9.1 %fusion.39 = f32[4,2,320,64]{2,3,1,0:T(8,128)S(1)} fusion(f32[4,1,320,1280]{3,2,1,0:T(8,128)} %get-tuple-element.236, f32[4,1,320,1280]{3,2,1,0:T(8,128)S(1)} %get-tuple-element.235, s32[1280]{0:T(1024)S(1)} %add_select_fusion.1), kind=kOutput, calls=%fused_computation.50 | convolution fusion | flops 2519941120 | bytes 13767680 | tf_op jit(solution)/shard_map/dcar,rm->dcam/dot_general | solution.py:176
  (167 shorter events, 95.7 us)
Async XLA Ops:
  7.2 88.4 %all-reduce.3.cloned.1.call-start = ((), (), s32[]{:S(2)}) async-start(), calls=%async_computation | async-start | bytes 3932160 | tf_op jit(solution)/shard_map/psum | solution.py:22
  8.6 18.6 %collective-permute-start = (bf16[4,2,32,1280]{3,2,1,0:T(8,128)(2,1)S(1)}, bf16[4,2,32,1280]{3,2,1,0:T(8,128)(2,1)}, u32[]{:S(2)}, u32[]{:S(2)}) collective-permute-start(bf16[4,2,32,1280]{3,2,1,0:T(8,128)(2,1)S(1)} %get-tuple-element.237), channel_id=1, source_target_pairs={{0,1},{1,2},{2,3},{3,4},{4,5},{5,6},{6,7},{8,9},{9,10},{10,11},{11... | collective-permute-start | bytes 1966088 | tf_op jit(solution)/shard_map/ppermute | solution.py:30
  10.6 19.7 %collective-permute-start.1 = (bf16[4,2,32,1280]{3,2,1,0:T(8,128)(2,1)S(1)}, bf16[4,2,32,1280]{3,2,1,0:T(8,128)(2,1)}, u32[]{:S(2)}, u32[]{:S(2)}) collective-permute-start(bf16[4,2,32,1280]{3,2,1,0:T(8,128)(2,1)S(1)} %get-tuple-element.238), channel_id=1, source_target_pairs={{1,0},{2,1},{3,2},{4,3},{5,4},{6,5},{7,6},{9,8},{10,9},{11,10},{12... | collective-permute-start | bytes 1966088 | tf_op jit(solution)/shard_map/ppermute | solution.py:33
  24.1 3.1 copy-start.2
  375.8 3.4 copy-start.3
  383.7 4.2 copy-start
  383.7 4.2 copy-start.1
Sparse Core Ops, SparseCore 0:
  27.3 68.2 all-reduce.2
where the time goes:
time: 426 us; the launch traced here: 421 us
  local copies, waits for them, and re-layouts  202 us (47%)
  other arithmetic  77.3 us (18%)
  matrix products  70.1 us (16%)
  waiting for transfers between devices  51.4 us (12%)
  between operations  14.3 us (3%)
  starting transfers between devices  5.6 us (1%)
    dot_general x5, matrix products, process(): jnp.einsum('dcwib,dwbj->dciwj', shifted, pick_cols, preferred_element_typ...  51.5 us
    psum x1, waiting for transfers between devices, broadcast(): return lax.psum(jnp.where(mine, x, jnp.zeros_like(x)), axis)  51.4 us
    while x10, local copies, waits for them, and re-layouts  50.4 us
    dynamic_update_slice x5, local copies, waits for them, and re-layouts, process(): lax.dynamic_update_slice_in_dim(ref_buffer, ref_rows, tile_line_number *...  40.9 us
    reduce_sum x5, other arithmetic, process(): covariance = jnp.mean(ref_dev[None] * sec_dev, axis=(1, 3))  21.4 us
    reduce_sum x5, other arithmetic, process(): sec_dev = sec_amp - jnp.mean(sec_amp, axis=(1, 3), keepdims=True)  18.6 us
    convert_element_type x5, local copies, waits for them, and re-layouts, process(): moved.astype(jnp.bfloat16).reshape(epochs_present, 2, WIN, pixel_values)  17.6 us
    dynamic_slice x5, local copies, waits for them, and re-layouts, process(): lax.dynamic_slice_in_dim(padded, tile_line_number * WIN, WIN + 2 * MARGIN...  16.8 us
  transfers between devices with their start and end apart: 3, of which 1 were waited for; matrix products, arithmetic and copies ran while one was open for 7% of the time, Pallas kernels for 0%

commit v1 on v0

v1 whole, which is shorter than its diff:
```python
import functools

import jax
import jax.numpy as jnp
import numpy as np
from jax import lax
from jax.experimental import pallas as pl
from jax.experimental.pallas import tpu as pltpu
from jax.sharding import PartitionSpec as P

WIN = 64
MARGIN = 32
LOOK_AZ = 5
LOOK_RG = 20
PATCH = 32
LANES = 128

VAR_EPS = 1e-05
RMS_EPS = 1e-06
TINY = 1e-37

F32 = jnp.float32
BF16 = jnp.bfloat16


def tables(lines, samples):
    turns = np.outer(np.arange(PATCH), np.arange(PATCH)) % PATCH
    angles = turns * (2.0 * np.pi / PATCH)
    two = np.eye(2)
    cosine = np.kron(two, np.cos(angles))
    sine = np.kron(two, np.sin(angles))
    rows_fwd = np.block([[cosine, sine], [-sine, cosine]])
    cols_fwd = np.block([[cosine, -sine], [sine, cosine]])
    dft = np.stack([rows_fwd, cols_fwd]).astype(np.float32)
    near = np.abs(np.arange(PATCH)[:, None] - np.arange(PATCH)[None, :])
    circular = np.minimum(near, PATCH - near) <= 1
    four = np.eye(LANES // PATCH)
    half = np.kron(np.eye(2), np.ones((WIN, WIN)))
    blocks = np.stack(
        [half, np.kron(four, circular), np.kron(four, np.ones((PATCH, PATCH)))]
    ).astype(np.float32)
    az_pool = (
        np.arange(lines // LOOK_AZ)[:, None] == np.arange(lines)[None, :] // LOOK_AZ
    ).astype(np.float32)
    rg_pool = (
        np.arange(samples)[:, None] // LOOK_RG == np.arange(samples // LOOK_RG)[None, :]
    ).astype(np.float32)
    rg_pool = np.concatenate([rg_pool, rg_pool], axis=0)
    return (
        jnp.asarray(dft),
        jnp.asarray(blocks, BF16),
        jnp.asarray(az_pool, BF16),
        jnp.asarray(rg_pool, BF16),
    )


def dot(a, b):
    return jnp.dot(a, b, preferred_element_type=F32)


def dot_high(a, b):
    return jnp.dot(a, b, preferred_element_type=F32, precision=lax.Precision.HIGHEST)


def split(x):
    high = x.astype(BF16)
    return high, (x - high.astype(F32)).astype(BF16)


def dot_right(x, ones):
    high, low = split(x)
    return dot(high, ones) + dot(low, ones)


def dot_left(ones, x):
    high, low = split(x)
    return dot(ones, high) + dot(ones, low)


def root(x):
    return x * lax.rsqrt(jnp.maximum(x, TINY))


def window_row(p, sizes, at_ref, ct_ref, pr_ref, ref_chunk, blk_ref, rgp_ref, wide, band, prod, pooled, stats, sims):
    dates, lines, strips = sizes
    for m in range(strips):
        cols = slice(m * LANES, (m + 1) * LANES)
        real = ref_chunk(0, cols)
        imag = ref_chunk(1, cols)
        band[0, m] = real
        band[1, m] = imag
        amp = root(real * real + imag * imag).reshape(WIN // 8, 8, LANES)
        mean = jnp.sum(amp, axis=0) * (8.0 / WIN)
        dev = amp - mean[None]
        band[2, m] = dev.reshape(WIN, LANES)
        stats[0, m, dates] = mean
        stats[1, m, dates] = jnp.sum(dev * dev, axis=0)

    def one_date(d, carry):
        lane = lax.broadcasted_iota(jnp.int32, (WIN, LANES), 1)
        first = lane < WIN
        near_low = lane < LANES - MARGIN
        near_high = lane < MARGIN
        present = pr_ref[d, p]
        for m in range(strips):
            rows = []
            turns = []
            for q in (2 * m, 2 * m + 1):
                start = jnp.where(
                    present != 0, p * WIN + MARGIN + at_ref[d, p, q], lines + 2 * MARGIN
                )
                rows.append(pl.ds(start, WIN))
                turns.append((LANES - ct_ref[d, p, q]) % LANES)
            part = []
            for c in range(2):
                even = wide[d, c, m, rows[0], :]
                below = wide[d, c, m - 1, rows[0], :] if m > 0 else jnp.zeros_like(even)
                odd = wide[d, c, m, rows[1], :]
                above = wide[d, c, m + 1, rows[1], :] if m + 1 < strips else jnp.zeros_like(odd)
                even = pltpu.roll(jnp.where(near_low, even, below), turns[0], 1)
                odd = pltpu.roll(jnp.where(near_high, above, odd), turns[1], 1)
                part.append(jnp.where(first, even, odd))
            sr, si = part
            amp = root(sr * sr + si * si).reshape(WIN // 8, 8, LANES)
            mean = jnp.sum(amp, axis=0) * (8.0 / WIN)
            dev = amp - mean[None]
            stats[0, m, d] = mean
            stats[1, m, d] = jnp.sum(dev * dev, axis=0)
            stats[2, m, d] = jnp.sum(dev * band[2, m].reshape(WIN // 8, 8, LANES), axis=0)
            rr = band[0, m]
            ri = band[1, m]
            for c, value in enumerate((rr * sr + ri * si, ri * sr - rr * si)):
                high, low = split(value)
                prod[d, c, :, m * LANES : (m + 1) * LANES] = high
                prod[d, c, :, (strips + m) * LANES : (strips + m + 1) * LANES] = low
        return carry

    lax.fori_loop(0, dates, one_date, 0)
    width = 2 * strips * LANES
    sums = dot(prod[...].reshape(dates * 2 * WIN, width), rgp_ref[...])
    pooled[:, :, pl.ds(pl.multiple_of(p * WIN, WIN), WIN), :] = sums.reshape(dates, 2, WIN, -1)

    half = blk_ref[0]

    def total(x):
        flat = x.reshape(-1, LANES)
        return jnp.sum(dot_right(flat, half).reshape(-1, 8, LANES), axis=1, keepdims=True)

    count = 8.0 * WIN
    means = stats[0].reshape(strips * (dates + 1), 8, LANES)
    away = means - total(means) * (1.0 / count)
    spread = stats[1].reshape(strips * (dates + 1), 8, LANES)
    var = total(spread + (WIN / 8.0) * (away * away)) * (1.0 / (WIN * WIN))
    away = away.reshape(strips, dates + 1, 8, LANES)
    var = var.reshape(strips, dates + 1, 1, LANES)
    joint = stats[2][:, :dates] + (WIN / 8.0) * (away[:, :dates] * away[:, dates:])
    cov = total(joint).reshape(strips, dates, 1, LANES) * (1.0 / (WIN * WIN))
    corr = cov / jnp.sqrt((var[:, dates:] + VAR_EPS) * (var[:, :dates] + VAR_EPS))
    lane = lax.broadcasted_iota(jnp.int32, (dates, 1, LANES), 2)
    found = jnp.zeros((dates, 1, LANES), F32)
    for m in range(strips):
        here = corr[m]
        other = pltpu.roll(here.reshape(dates, LANES), WIN, 1).reshape(dates, 1, LANES)
        left = jnp.where(lane < WIN, here, other)
        right = jnp.where(lane < WIN, other, here)
        found = jnp.where(lane == 2 * m, left, jnp.where(lane == 2 * m + 1, right, found))
    sims[p] = found


def goldstein(dates, out_ref, dft_ref, blk_ref, azp_ref, pooled):
    az_pool = azp_ref[...]
    looks_az = az_pool.shape[0]
    rows_fwd = dft_ref[0]
    cols_fwd = dft_ref[1]

    def rows_to_cols(x):
        return jnp.concatenate([x[:looks_az], x[looks_az:]], axis=1)

    turned = []
    for d in range(dates):
        z = jnp.concatenate([dot_left(az_pool, pooled[d, c]) for c in range(2)], axis=0)
        turned.append(rows_to_cols(dot_high(rows_fwd, z)))
    spectrum = dot_high(jnp.concatenate(turned, axis=0), cols_fwd)
    squares = spectrum * spectrum
    magnitude = root(squares + pltpu.roll(squares, WIN, 1))
    smooth = dot_right(magnitude, blk_ref[1]).reshape(-1, PATCH, LANES)
    smooth = (
        smooth
        + jnp.concatenate([smooth[:, 1:], smooth[:, :1]], axis=1)
        + jnp.concatenate([smooth[:, -1:], smooth[:, :-1]], axis=1)
    ).reshape(spectrum.shape)
    weighted = spectrum * root(smooth * (1.0 / 9.0))
    turned = []
    for d in range(dates):
        w = weighted[d * looks_az : (d + 1) * looks_az]
        w = jnp.concatenate([w[:, :WIN], w[:, WIN:]], axis=0)
        turned.append(rows_to_cols(dot_high(cols_fwd, w)))
    back = dot_high(jnp.concatenate(turned, axis=0), rows_fwd)
    squares = back * back
    power = dot_right(squares + pltpu.roll(squares, WIN, 1), blk_ref[2]).reshape(-1, PATCH, LANES)
    power = jnp.sum(power, axis=1, keepdims=True) * (1.0 / (PATCH * PATCH))
    scaled = back.reshape(-1, PATCH, LANES) * lax.rsqrt(power + RMS_EPS)
    scaled = scaled.reshape(back.shape)
    for d in range(dates):
        rows = scaled[d * looks_az : (d + 1) * looks_az]
        out_ref[d, 0] = rows[:, :WIN]
        out_ref[d, 1] = rows[:, WIN:]


def kernel(
    at_ref, ct_ref, pr_ref, img_ref, low_ref, high_ref, ref_ref, dft_ref, blk_ref, azp_ref, rgp_ref,
    sim_ref, out_ref,
    wide, band, prod, pooled, stats, sims,
):
    dates, _, lines, samples = img_ref.shape
    strips = samples // LANES
    rows = lines // WIN

    def widen(i, carry):
        d = i // 2
        c = i % 2
        for m in range(strips):
            cols = slice(m * LANES, (m + 1) * LANES)
            wide[d, c, m, 0:MARGIN, :] = low_ref[d, c, :, cols].astype(F32)
            wide[d, c, m, MARGIN : MARGIN + lines, :] = img_ref[d, c, :, cols].astype(F32)
            wide[d, c, m, MARGIN + lines : 2 * MARGIN + lines, :] = high_ref[d, c, :, cols].astype(F32)
            wide[d, c, m, 2 * MARGIN + lines : 2 * MARGIN + lines + WIN, :] = jnp.zeros((WIN, LANES), F32)
        return carry

    lax.fori_loop(0, 2 * dates, widen, 0)
    stats[2] = jnp.zeros(stats.shape[1:], F32)

    def row(p, carry):
        def ref_chunk(c, cols):
            return ref_ref[c, pl.ds(pl.multiple_of(p * WIN, WIN), WIN), cols].astype(F32)

        window_row(
            p, (dates, lines, strips), at_ref, ct_ref, pr_ref, ref_chunk, blk_ref, rgp_ref,
            wide, band, prod, pooled, stats, sims,
        )
        return carry

    lax.fori_loop(0, rows, row, 0)
    for p in range(rows):
        sim_ref[:, p : p + 1, :] = sims[p][:, :, : sim_ref.shape[2]]
    goldstein(dates, out_ref, dft_ref, blk_ref, azp_ref, pooled)


def broadcast(x, axis, root_index):
    mine = lax.axis_index(axis) == root_index
    return lax.psum(jnp.where(mine, x, jnp.zeros_like(x)), axis)


def on_device(image, along, cross, present):
    dates, _, lines, samples = image.shape
    strips = samples // LANES
    rows = lines // WIN
    ref = broadcast(image[0], "date", 0)
    count = lax.axis_size("az")
    forward = [(i, i + 1) for i in range(count - 1)]
    backward = [(b, a) for a, b in forward]
    low = lax.ppermute(image[:, :, lines - MARGIN :], "az", forward)
    high = lax.ppermute(image[:, :, :MARGIN], "az", backward)
    smem = pl.BlockSpec(memory_space=pltpu.SMEM)
    vmem = pl.BlockSpec(memory_space=pltpu.VMEM)
    return pl.pallas_call(
        kernel,
        out_shape=(
            jax.ShapeDtypeStruct((dates, rows, samples // WIN), F32),
            jax.ShapeDtypeStruct((dates, 2, lines // LOOK_AZ, samples // LOOK_RG), F32),
        ),
        in_specs=[smem] * 3 + [vmem] * 8,
        out_specs=(vmem, vmem),
        scratch_shapes=[
            pltpu.VMEM((dates, 2, strips, lines + 2 * MARGIN + WIN, LANES), F32),
            pltpu.VMEM((3, strips, WIN, LANES), F32),
            pltpu.VMEM((dates, 2, WIN, 2 * samples), BF16),
            pltpu.VMEM((dates, 2, lines, samples // LOOK_RG), F32),
            pltpu.VMEM((3, strips, dates + 1, 8, LANES), F32),
            pltpu.VMEM((rows, dates, 1, LANES), F32),
        ],
        compiler_params=pltpu.CompilerParams(vmem_limit_bytes=56 * 1024 * 1024),
    )(along, cross, present, image, low, high, ref, *tables(lines, samples))


def solution(mesh):
    placed = (
        P("date", None, "az", None),
        P("date", "az", None),
        P("date", "az", None),
        P("date", "az"),
    )
    return jax.shard_map(
        on_device,
        mesh=mesh,
        in_specs=placed,
        out_specs=(P("date", "az", None), P("date", None, "az", None)),
        check_vma=False,
    )
```

time: 426 us -> 110 us (0.26)
  local copies, waits for them, and re-layouts: 202 us -> 3.94 us
  other arithmetic: 77.3 us -> 2.71 us
  matrix products: 70.1 us -> 0 us
  Pallas kernels: 0 us -> 25.6 us
  waiting for transfers between devices: 51.4 us -> 55.8 us
    dot_general x23 -> x0, matrix products: 70.1 us -> none  [the longest x5 51.5 us: process(): jnp.einsum('dcwib,dwbj->dciwj', shifted, pick_cols, preferred_element_typ...]
    dynamic_update_slice x10 -> x0, local copies, waits for them, and re-layouts: 53.3 us -> none  [the longest x5 40.9 us: process(): lax.dynamic_update_slice_in_dim(ref_buffer, ref_rows, tile_line_number *...]
    while x11 -> x0, local copies, waits for them, and re-layouts: 50.5 us -> none
    reduce_sum x30 -> x0, other arithmetic: 45 us -> none  [the longest x5 21.4 us: process(): covariance = jnp.mean(ref_dev[None] * sec_dev, axis=(1, 3))]
    pallas_call x0 -> x1, Pallas kernels: none -> 25.6 us  [on_device(): pl.pallas_call(kernel, out_shape=(jax.ShapeDtypeStruct((dates, rows, samp...]
    convert_element_type x5 -> x0, local copies, waits for them, and re-layouts: 17.6 us -> none  [process(): moved.astype(jnp.bfloat16).reshape(epochs_present, 2, WIN, pixel_values)]
    dynamic_slice x5 -> x0, local copies, waits for them, and re-layouts: 16.8 us -> none  [process(): lax.dynamic_slice_in_dim(padded, tile_line_number * WIN, WIN + 2 * MARGIN...]
    slice x11 -> x1, local copies, waits for them, and re-layouts: 15.7 us -> 1.4 us  [on_device(): high = lax.ppermute(image[:, :, :MARGIN], 'az', backward)]
  transfers between devices with their start and end apart: 3 -> 3, of which waited for: 1 -> 3; matrix products, arithmetic and copies ran while one was open for 7% -> 2% of each run, Pallas kernels for 0% -> 0%
where the time goes in v1:
time: 110 us; the launch traced here: 108 us
  waiting for transfers between devices  55.8 us (51%)
  Pallas kernels  25.6 us (23%)
  between operations  14.1 us (13%)
  starting transfers between devices  5.6 us (5%)
  local copies, waits for them, and re-layouts  3.94 us (4%)
  other arithmetic  2.71 us (2%)
    psum x1, waiting for transfers between devices, broadcast(): return lax.psum(jnp.where(mine, x, jnp.zeros_like(x)), axis)  49 us
    pallas_call x1, Pallas kernels, on_device(): pl.pallas_call(kernel, out_shape=(jax.ShapeDtypeStruct((dates, rows, samp...  25.6 us
    ppermute x1, waiting for transfers between devices, on_device(): low = lax.ppermute(image[:, :, lines - MARGIN:], 'az', forward)  5.11 us
    ppermute x1, starting transfers between devices, on_device(): high = lax.ppermute(image[:, :, :MARGIN], 'az', backward)  3.64 us
    select_n x1, other arithmetic, broadcast(): return lax.psum(jnp.where(mine, x, jnp.zeros_like(x)), axis)  2.71 us
  transfers between devices with their start and end apart: 3, of which 3 were waited for; matrix products, arithmetic and copies ran while one was open for 2% of the time, Pallas kernels for 0%

profile of v1, /device:TPU:28, one launch (start us, length us, event | category | flops | bytes accessed | tf_op | source)
XLA Modules:
  0.0 107.7 jit_solution(1506888420262717008)
XLA Ops:
  7.2 0.0 all-reduce.2.cloned.1.call-start
  7.2 2.7 %select_bitcast_fusion = bf16[2,320,1280]{2,1,0:T(8,128)(2,1)} fusion(bf16[4,2,320,1280]{3,2,1,0:T(8,128)(2,1)} %img_ref.1, pred[]{:T(512)S(6)} %eq.3), kind=kLoop, calls=%fused_computation | loop fusion | flops 819200 | bytes 3276801 | tf_op jit(solution)/shard_map/jit(_where)/select_n | solution.py:251
  9.9 0.0 all-reduce.2.cloned.1.call-update
  9.9 0.0 copy-start.2
  10.0 0.0 copy-start.3
  10.0 1.4 %fusion = (bf16[4,2,32,1280]{3,2,1,0:T(8,128)(2,1)S(1)}, bf16[4,2,32,1280]{3,2,1,0:T(8,128)(2,1)S(1)}) fusion(bf16[4,2,320,1280]{3,2,1,0:T(8,128)(2,1)} %img_ref.1), kind=kLoop, calls=%fused_computation.1 | loop fusion | bytes 2621440 | tf_op jit(solution)/shard_map/slice | solution.py:263
  11.4 1.9 %collective-permute-start = (bf16[4,2,32,1280]{3,2,1,0:T(8,128)(2,1)S(1)}, bf16[4,2,32,1280]{3,2,1,0:T(8,128)(2,1)S(1)}, u32[]{:S(2)}, u32[]{:S(2)}) collective-permute-start(bf16[4,2,32,1280]{3,2,1,0:T(8,128)(2,1)S(1)} %get-tuple-element.5), channel_id=1, source_target_pairs={{0,1},{1,2},{2,3},{3,4},{4,5},{5,6},{6,7},{8,9},{9,10},{10,11},{11... | collective-permute-start | bytes 1966088 | tf_op jit(solution)/shard_map/ppermute | solution.py:262
  13.3 3.6 %collective-permute-start.1 = (bf16[4,2,32,1280]{3,2,1,0:T(8,128)(2,1)S(1)}, bf16[4,2,32,1280]{3,2,1,0:T(8,128)(2,1)S(1)}, u32[]{:S(2)}, u32[]{:S(2)}) collective-permute-start(bf16[4,2,32,1280]{3,2,1,0:T(8,128)(2,1)S(1)} %get-tuple-element.4), channel_id=1, source_target_pairs={{1,0},{2,1},{3,2},{4,3},{5,4},{6,5},{7,6},{9,8},{10,9},{11,10},{12... | collective-permute-start | bytes 1966088 | tf_op jit(solution)/shard_map/ppermute | solution.py:263
  17.0 0.0 copy-done.2
  17.0 0.6 copy.10.at_ref
  17.6 0.0 copy-done.3
  17.6 0.6 copy.11.ct_ref
  18.2 5.1 %collective-permute-done.low_ref = bf16[4,2,32,1280]{3,2,1,0:T(8,128)(2,1)S(1)} collective-permute-done((bf16[4,2,32,1280]{3,2,1,0:T(8,128)(2,1)S(1)}, bf16[4,2,32,1280]{3,2,1,0:T(8,128)(2,1)S(1)}, u32[]{:S(2)}, u32[]{:S(2)}) %collective-permute-start) | collective-permute-done | bytes 655392 | tf_op jit(solution)/shard_map/ppermute | solution.py:262
  23.3 0.0 copy-start
  23.3 1.8 %collective-permute-done.1.high_ref = bf16[4,2,32,1280]{3,2,1,0:T(8,128)(2,1)S(1)} collective-permute-done((bf16[4,2,32,1280]{3,2,1,0:T(8,128)(2,1)S(1)}, bf16[4,2,32,1280]{3,2,1,0:T(8,128)(2,1)S(1)}, u32[]{:S(2)}, u32[]{:S(2)}) %collective-permute-start.1) | collective-permute-done | bytes 655392 | tf_op jit(solution)/shard_map/ppermute | solution.py:263
  25.0 0.0 copy-start.1
  25.0 49.0 %all-reduce.2.cloned.1.call-done.ref_ref = bf16[2,320,1280]{2,1,0:T(8,128)(2,1)} async-done(((bf16[2,320,1280]{2,1,0:T(8,128)(2,1)}), bf16[2,320,1280]{2,1,0:T(8,128)(2,1)}) %all-reduce.2.cloned.1.call-update) | async-done | bytes 1638416 | tf_op jit(solution)/shard_map/psum | solution.py:251
  74.0 0.0 copy-done
  74.0 0.0 copy-done.1
  74.0 25.6 %shard_map.95 = (f32[4,5,20]{2,1,0:T(8,128)}, f32[4,2,64,64]{3,2,1,0:T(8,128)}) custom-call(s32[4,5,20]{2,1,0:T(8,128)} %copy.10.at_ref, s32[4,5,20]{2,1,0:T(8,128)} %copy.11.ct_ref, s32[4,5]{1,0:T(4,128)} %pr_ref.1, bf16[4,2,320,1280]{3,2,1,0:T(8,128)(2,1)} %img_ref.1, bf16[4,2,32,1280]{3,2,1,0:T(8,128)(2,1)} %copy-done, ...), custom_call_target="tpu_custom_call" | custom-call | tf_op jit(solution)/shard_map/pallas_call | solution.py:266
  99.6 1.3 %copy.12 = f32[4,5,20]{2,0,1:T(4,128)} copy(f32[4,5,20]{2,1,0:T(8,128)} %get-tuple-element.2) | data formatting | bytes 3200 | tf_op jit(solution)/shard_map/pallas_call | solution.py:266
Async XLA Ops:
  7.2 66.8 %all-reduce.2.cloned.1.call-start = ((), (), s32[]{:S(2)}) async-start(), calls=%async_computation | async-start | bytes 3276800 | tf_op jit(solution)/shard_map/psum | solution.py:251
  9.9 7.0 %copy-start.2 = (s32[4,5,20]{2,0,1:T(4,128)S(1)}, s32[4,5,20]{2,0,1:T(4,128)}, u32[]{:S(2)}) copy-start(s32[4,5,20]{2,0,1:T(4,128)} %param.9) | copy-start | bytes 4804
  10.0 7.6 %copy-start.3 = (s32[4,5,20]{2,0,1:T(4,128)S(1)}, s32[4,5,20]{2,0,1:T(4,128)}, u32[]{:S(2)}) copy-start(s32[4,5,20]{2,0,1:T(4,128)} %param.10) | copy-start | bytes 4804
  11.4 11.9 %collective-permute-start = (bf16[4,2,32,1280]{3,2,1,0:T(8,128)(2,1)S(1)}, bf16[4,2,32,1280]{3,2,1,0:T(8,128)(2,1)S(1)}, u32[]{:S(2)}, u32[]{:S(2)}) collective-permute-start(bf16[4,2,32,1280]{3,2,1,0:T(8,128)(2,1)S(1)} %get-tuple-element.5), channel_id=1, source_target_pairs={{0,1},{1,2},{2,3},{3,4},{4,5},{5,6},{6,7},{8,9},{9,10},{10,11},{11... | collective-permute-start | bytes 1966088 | tf_op jit(solution)/shard_map/ppermute | solution.py:262
  13.3 11.7 %collective-permute-start.1 = (bf16[4,2,32,1280]{3,2,1,0:T(8,128)(2,1)S(1)}, bf16[4,2,32,1280]{3,2,1,0:T(8,128)(2,1)S(1)}, u32[]{:S(2)}, u32[]{:S(2)}) collective-permute-start(bf16[4,2,32,1280]{3,2,1,0:T(8,128)(2,1)S(1)} %get-tuple-element.4), channel_id=1, source_target_pairs={{1,0},{2,1},{3,2},{4,3},{5,4},{6,5},{7,6},{9,8},{10,9},{11,10},{12... | collective-permute-start | bytes 1966088 | tf_op jit(solution)/shard_map/ppermute | solution.py:263
  23.3 50.7 %copy-start = (bf16[4,2,32,1280]{3,2,1,0:T(8,128)(2,1)}, bf16[4,2,32,1280]{3,2,1,0:T(8,128)(2,1)S(1)}, u32[]{:S(2)}) copy-start(bf16[4,2,32,1280]{3,2,1,0:T(8,128)(2,1)S(1)} %collective-permute-done.low_ref) | copy-start | bytes 1966084
  25.0 49.0 %copy-start.1 = (bf16[4,2,32,1280]{3,2,1,0:T(8,128)(2,1)}, bf16[4,2,32,1280]{3,2,1,0:T(8,128)(2,1)S(1)}, u32[]{:S(2)}) copy-start(bf16[4,2,32,1280]{3,2,1,0:T(8,128)(2,1)S(1)} %collective-permute-done.1.high_ref) | copy-start | bytes 1966084
Sparse Core Ops, SparseCore 0:
  11.1 62.8 all-reduce.1

commit v2 on v1

--- a/solution.py
+++ b/solution.py
@@ -1,5 +1,3 @@
-import functools
-
 import jax
 import jax.numpy as jnp
 import numpy as np
@@ -14,6 +12,8 @@
 LOOK_RG = 20
 PATCH = 32
 LANES = 128
+PIECE = 16
+AHEAD = 8
 
 VAR_EPS = 1e-05
 RMS_EPS = 1e-06
@@ -81,7 +81,7 @@
     return x * lax.rsqrt(jnp.maximum(x, TINY))
 
 
-def window_row(p, sizes, at_ref, ct_ref, pr_ref, ref_chunk, blk_ref, rgp_ref, wide, band, prod, pooled, stats, sims):
+def window_row(p, sizes, at_ref, ct_ref, pr_ref, ref_chunk, blk_ref, rgp_ref, wide, band, prod, pooled, stats, sims, follow):
     dates, lines, strips = sizes
     for m in range(strips):
         cols = slice(m * LANES, (m + 1) * LANES)
@@ -97,6 +97,7 @@
         stats[1, m, dates] = jnp.sum(dev * dev, axis=0)
 
     def one_date(d, carry):
+        follow(d)
         lane = lax.broadcasted_iota(jnp.int32, (WIN, LANES), 1)
         first = lane < WIN
         near_low = lane < LANES - MARGIN
@@ -207,36 +208,191 @@
         out_ref[d, 1] = rows[:, WIN:]
 
 
+def ring_device(position, count):
+    half = count // 2
+    return jnp.where(position < half, 2 * position, 2 * (count - 1 - position) + 1)
+
+
 def kernel(
-    at_ref, ct_ref, pr_ref, img_ref, low_ref, high_ref, ref_ref, dft_ref, blk_ref, azp_ref, rgp_ref,
+    at_ref, ct_ref, pr_ref, img_ref, dft_ref, blk_ref, azp_ref, rgp_ref,
     sim_ref, out_ref,
-    wide, band, prod, pooled, stats, sims,
+    image, halo, ref, wide, band, prod, pooled, stats, sims,
+    image_sem, root_sem, halo_send, halo_recv, ref_send, ref_recv,
 ):
     dates, _, lines, samples = img_ref.shape
     strips = samples // LANES
     rows = lines // WIN
+    pieces = ref_send.shape[1]
+    height = lines // pieces
+    each = WIN // height
+    count = lax.axis_size("date")
+    az_count = lax.axis_size("az")
+    az = lax.axis_index("az")
+    mine = lax.axis_index("date")
+    position = jnp.where(mine % 2 == 0, mine // 2, count - 1 - mine // 2)
+    after = ring_device((position + 1) % count, count)
+    before = ring_device((position + count - 1) % count, count)
+    hops = (position, (count - position) % count)
+    targets = (after, before)
+    mesh_ids = pl.DeviceIdType.MESH
+
+    def load(i):
+        d = i // 2
+        c = i % 2
+        return pltpu.make_async_copy(img_ref.at[d, c], image.at[d, c], image_sem.at[i])
+
+    for i in range(2 * dates):
+        load(i).start()
+    own = pltpu.make_async_copy(img_ref.at[0], ref, root_sem)
+
+    @pl.when(mine == 0)
+    def _():
+        own.start()
+
+    barrier = pltpu.get_barrier_semaphore()
+    for target in targets:
+        pl.semaphore_signal(barrier, inc=1, device_id={"date": target}, device_id_type=mesh_ids)
+
+    @pl.when(az > 0)
+    def _():
+        pl.semaphore_signal(barrier, inc=1, device_id={"az": az - 1}, device_id_type=mesh_ids)
+
+    @pl.when(az < az_count - 1)
+    def _():
+        pl.semaphore_signal(barrier, inc=1, device_id={"az": az + 1}, device_id_type=mesh_ids)
+
+    peers = 2 + jnp.where(az > 0, 1, 0) + jnp.where(az < az_count - 1, 1, 0)
+    pl.semaphore_wait(barrier, peers)
+
+    def row_of(s):
+        return jnp.where(s < rows - 2, s + 1, jnp.where(s == rows - 2, 0, rows - 1))
+
+    def piece_rows(j):
+        return pl.ds(pl.multiple_of(row_of(j // each) * WIN + (j % each) * height, height), height)
+
+    def relay(c, j, first):
+        at = piece_rows(j)
+        return pltpu.make_async_remote_copy(
+            src_ref=img_ref.at[0, c, at] if first else ref.at[c, at],
+            dst_ref=ref.at[c, at],
+            send_sem=ref_send.at[c, j],
+            recv_sem=ref_recv.at[c, j],
+            device_id={"date": targets[c]},
+            device_id_type=mesh_ids,
+        )
+
+    def launch(j):
+        for c in range(2):
+            relay(c, j, True).start()
+
+    def pass_on(j):
+        for c in range(2):
+            @pl.when(hops[c] > 0)
+            def _():
+                relay(c, j, False).wait_recv()
+
+            @pl.when((hops[c] > 0) & (hops[c] < count - 1))
+            def _():
+                relay(c, j, False).start()
+
+        @pl.when((mine == 0) & (j + AHEAD < pieces))
+        def _():
+            launch(j + AHEAD)
+
+    @pl.when(mine == 0)
+    def _():
+        for j in range(AHEAD):
+            launch(j)
+
+    def edge(k):
+        start = 0 if k else lines - MARGIN
+        return pltpu.make_async_remote_copy(
+            src_ref=img_ref.at[:, :, pl.ds(start, MARGIN)],
+            dst_ref=halo.at[k],
+            send_sem=halo_send.at[k],
+            recv_sem=halo_recv.at[k],
+            device_id={"az": az - 1 if k else az + 1},
+            device_id_type=mesh_ids,
+        )
+
+    sends = (az < az_count - 1, az > 0)
+    takes = (az > 0, az < az_count - 1)
+    for k in range(2):
+        @pl.when(sends[k])
+        def _():
+            edge(k).start()
 
     def widen(i, carry):
         d = i // 2
         c = i % 2
+        load(i).wait()
         for m in range(strips):
             cols = slice(m * LANES, (m + 1) * LANES)
-            wide[d, c, m, 0:MARGIN, :] = low_ref[d, c, :, cols].astype(F32)
-            wide[d, c, m, MARGIN : MARGIN + lines, :] = img_ref[d, c, :, cols].astype(F32)
-            wide[d, c, m, MARGIN + lines : 2 * MARGIN + lines, :] = high_ref[d, c, :, cols].astype(F32)
+            wide[d, c, m, MARGIN : MARGIN + lines, :] = image[d, c, :, cols].astype(F32)
             wide[d, c, m, 2 * MARGIN + lines : 2 * MARGIN + lines + WIN, :] = jnp.zeros((WIN, LANES), F32)
+
+        @pl.when(i >= 2 * dates - each)
+        def _():
+            pass_on(i - (2 * dates - each))
+
         return carry
 
     lax.fori_loop(0, 2 * dates, widen, 0)
+
+    @pl.when(mine == 0)
+    def _():
+        own.wait()
+
     stats[2] = jnp.zeros(stats.shape[1:], F32)
 
-    def row(p, carry):
+    def fringe(k):
+        first = MARGIN + lines if k else 0
+
+        @pl.when(takes[k])
+        def _():
+            edge(k).wait_recv()
+
+            def convert(i, carry):
+                d = i // 2
+                c = i % 2
+                for m in range(strips):
+                    cols = slice(m * LANES, (m + 1) * LANES)
+                    wide[d, c, m, first : first + MARGIN, :] = halo[k, d, c, :, cols].astype(F32)
+                return carry
+
+            lax.fori_loop(0, 2 * dates, convert, 0)
+
+        @pl.when(jnp.logical_not(takes[k]))
+        def _():
+            def clear(i, carry):
+                for m in range(strips):
+                    wide[i // 2, i % 2, m, first : first + MARGIN, :] = jnp.zeros((MARGIN, LANES), F32)
+                return carry
+
+            lax.fori_loop(0, 2 * dates, clear, 0)
+
+    def row(s, carry):
+        @pl.when(s == rows - 2)
+        def _():
+            for k in range(2):
+                fringe(k)
+
+        p = row_of(s)
+
         def ref_chunk(c, cols):
-            return ref_ref[c, pl.ds(pl.multiple_of(p * WIN, WIN), WIN), cols].astype(F32)
+            return ref[c, pl.ds(pl.multiple_of(p * WIN, WIN), WIN), cols].astype(F32)
+
+        def follow(d):
+            for e in range(each // dates if each >= dates else 1):
+                j = (s + 1) * each + d * max(each // dates, 1) + e
+
+                @pl.when((s < rows - 1) & (j < (s + 2) * each))
+                def _():
+                    pass_on(j)
 
         window_row(
             p, (dates, lines, strips), at_ref, ct_ref, pr_ref, ref_chunk, blk_ref, rgp_ref,
-            wide, band, prod, pooled, stats, sims,
+            wide, band, prod, pooled, stats, sims, follow,
         )
         return carry
 
@@ -245,42 +401,58 @@
         sim_ref[:, p : p + 1, :] = sims[p][:, :, : sim_ref.shape[2]]
     goldstein(dates, out_ref, dft_ref, blk_ref, azp_ref, pooled)
 
-
-def broadcast(x, axis, root_index):
-    mine = lax.axis_index(axis) == root_index
-    return lax.psum(jnp.where(mine, x, jnp.zeros_like(x)), axis)
+    for c in range(2):
+        @pl.when(hops[c] < count - 1)
+        def _():
+            def drain(j, carry):
+                relay(c, j, False).wait_send()
+                return carry
+
+            lax.fori_loop(0, pieces, drain, 0)
+
+    for k in range(2):
+        @pl.when(sends[k])
+        def _():
+            edge(k).wait_send()
 
 
 def on_device(image, along, cross, present):
     dates, _, lines, samples = image.shape
     strips = samples // LANES
     rows = lines // WIN
-    ref = broadcast(image[0], "date", 0)
-    count = lax.axis_size("az")
-    forward = [(i, i + 1) for i in range(count - 1)]
-    backward = [(b, a) for a, b in forward]
-    low = lax.ppermute(image[:, :, lines - MARGIN :], "az", forward)
-    high = lax.ppermute(image[:, :, :MARGIN], "az", backward)
+    pieces = lines // PIECE
     smem = pl.BlockSpec(memory_space=pltpu.SMEM)
     vmem = pl.BlockSpec(memory_space=pltpu.VMEM)
+    dma = pltpu.SemaphoreType.DMA
     return pl.pallas_call(
         kernel,
         out_shape=(
             jax.ShapeDtypeStruct((dates, rows, samples // WIN), F32),
             jax.ShapeDtypeStruct((dates, 2, lines // LOOK_AZ, samples // LOOK_RG), F32),
         ),
-        in_specs=[smem] * 3 + [vmem] * 8,
+        in_specs=[smem] * 3 + [pl.BlockSpec(memory_space=pl.ANY)] + [vmem] * 4,
         out_specs=(vmem, vmem),
         scratch_shapes=[
+            pltpu.VMEM((dates, 2, lines, samples), BF16),
+            pltpu.VMEM((2, dates, 2, MARGIN, samples), BF16),
+            pltpu.VMEM((2, lines, samples), BF16),
             pltpu.VMEM((dates, 2, strips, lines + 2 * MARGIN + WIN, LANES), F32),
             pltpu.VMEM((3, strips, WIN, LANES), F32),
             pltpu.VMEM((dates, 2, WIN, 2 * samples), BF16),
             pltpu.VMEM((dates, 2, lines, samples // LOOK_RG), F32),
             pltpu.VMEM((3, strips, dates + 1, 8, LANES), F32),
             pltpu.VMEM((rows, dates, 1, LANES), F32),
+            dma((2 * dates,)),
+            dma(()),
+            dma((2,)),
+            dma((2,)),
+            dma((2, pieces)),
+            dma((2, pieces)),
         ],
-        compiler_params=pltpu.CompilerParams(vmem_limit_bytes=56 * 1024 * 1024),
-    )(along, cross, present, image, low, high, ref, *tables(lines, samples))
+        compiler_params=pltpu.CompilerParams(
+            vmem_limit_bytes=56 * 1024 * 1024, collective_id=0, has_side_effects=True
+        ),
+    )(along, cross, present, image, *tables(lines, samples))
 
 
 def solution(mesh):

time: 110 us -> 276 us (2.51)
  Pallas kernels: 25.6 us -> 269 us
  waiting for transfers between devices: 55.8 us -> 0 us
  between operations: 14.1 us -> 0.64 us
  starting transfers between devices: 5.6 us -> 0 us
    pallas_call x1, Pallas kernels: 25.6 us -> 269 us  [on_device(): pl.pallas_call(kernel, out_shape=(jax.ShapeDtypeStruct((dates, rows, samp...]
    psum x1 -> x0, waiting for transfers between devices: 49 us -> none  [broadcast(): return lax.psum(jnp.where(mine, x, jnp.zeros_like(x)), axis)]
    ppermute x2 -> x0, waiting for transfers between devices: 6.86 us -> none  [the longest x1 5.11 us: on_device(): low = lax.ppermute(image[:, :, lines - MARGIN:], 'az', forward)]
    ppermute x2 -> x0, starting transfers between devices: 5.56 us -> none  [the longest x1 3.64 us: on_device(): high = lax.ppermute(image[:, :, :MARGIN], 'az', backward)]
    unnamed x10 -> x3, local copies, waits for them, and re-layouts: 1.22 us -> 4.28 us
  transfers between devices with their start and end apart: 3 -> 0, of which waited for: 3 -> 0; matrix products, arithmetic and copies ran while one was open for 2% -> 0% of each run, Pallas kernels for 0% -> 0%
where the time goes in v2:
time: 276 us; the launch traced here: 275 us
  Pallas kernels  269 us (97%)
  local copies, waits for them, and re-layouts  5.6 us (2%)
    pallas_call x1, Pallas kernels, on_device(): pl.pallas_call(kernel, out_shape=(jax.ShapeDtypeStruct((dates, rows, samp...  269 us

profile of v2, /device:TPU:28, one launch (start us, length us, event | category | flops | bytes accessed | tf_op | source)
XLA Modules:
  0.0 275.4 jit_solution(12103967540201759971)
XLA Ops:
  0.6 1.3 copy.10.at_ref
  1.9 1.3 copy.11.ct_ref
  3.2 269.1 %shard_map.95 = (f32[4,5,20]{2,1,0:T(8,128)}, f32[4,2,64,64]{3,2,1,0:T(8,128)}) custom-call(s32[4,5,20]{2,1,0:T(8,128)} %copy.10.at_ref, s32[4,5,20]{2,1,0:T(8,128)} %copy.11.ct_ref, s32[4,5]{1,0:T(4,128)} %pr_ref.1, bf16[4,2,320,1280]{3,2,1,0:T(8,128)(2,1)} %img_ref.1, f32[2,128,128]{2,1,0:T(8,128)} %constant.8.clone.dft_ref, ...), custom_call_target="tpu_custom_call" | custom-call | tf_op jit(solution)/shard_map/pallas_call | solution.py:427
  272.4 1.3 copy.12
  273.7 1.7 copy.14

commit v3 on v2

--- a/solution.py
+++ b/solution.py
@@ -14,6 +14,7 @@
 LANES = 128
 PIECE = 16
 AHEAD = 8
+LAG = 3
 
 VAR_EPS = 1e-05
 RMS_EPS = 1e-06
@@ -285,19 +286,22 @@
         for c in range(2):
             relay(c, j, True).start()
 
-    def pass_on(j):
+    def slot(t):
         for c in range(2):
-            @pl.when(hops[c] > 0)
+            j = t - (hops[c] - 1) * LAG
+            here = (hops[c] > 0) & (j >= 0) & (j < pieces)
+
+            @pl.when(here)
             def _():
                 relay(c, j, False).wait_recv()
 
-            @pl.when((hops[c] > 0) & (hops[c] < count - 1))
+            @pl.when(here & (hops[c] < count - 1))
             def _():
                 relay(c, j, False).start()
 
-        @pl.when((mine == 0) & (j + AHEAD < pieces))
-        def _():
-            launch(j + AHEAD)
+        @pl.when((mine == 0) & (t + AHEAD < pieces))
+        def _():
+            launch(t + AHEAD)
 
     @pl.when(mine == 0)
     def _():
@@ -331,13 +335,20 @@
             wide[d, c, m, MARGIN : MARGIN + lines, :] = image[d, c, :, cols].astype(F32)
             wide[d, c, m, 2 * MARGIN + lines : 2 * MARGIN + lines + WIN, :] = jnp.zeros((WIN, LANES), F32)
 
-        @pl.when(i >= 2 * dates - each)
-        def _():
-            pass_on(i - (2 * dates - each))
+        @pl.when(i < early)
+        def _():
+            slot(i)
 
         return carry
 
+    early = each + (count - 2) * LAG
     lax.fori_loop(0, 2 * dates, widen, 0)
+
+    def catch_up(t, carry):
+        slot(t)
+        return carry
+
+    lax.fori_loop(2 * dates, max(2 * dates, early), catch_up, 0)
 
     @pl.when(mine == 0)
     def _():
@@ -383,12 +394,13 @@
             return ref[c, pl.ds(pl.multiple_of(p * WIN, WIN), WIN), cols].astype(F32)
 
         def follow(d):
-            for e in range(each // dates if each >= dates else 1):
-                j = (s + 1) * each + d * max(each // dates, 1) + e
-
-                @pl.when((s < rows - 1) & (j < (s + 2) * each))
+            share = -(-each // dates)
+            for e in range(share):
+                k = d * share + e
+
+                @pl.when((s < rows - 1) & (k < each))
                 def _():
-                    pass_on(j)
+                    slot(early + s * each + k)
 
         window_row(
             p, (dates, lines, strips), at_ref, ct_ref, pr_ref, ref_chunk, blk_ref, rgp_ref,

time: 276 us -> 50.7 us (0.18)
  Pallas kernels: 269 us -> 43.8 us
    pallas_call x1, Pallas kernels: 269 us -> 43.8 us  [on_device(): pl.pallas_call(kernel, out_shape=(jax.ShapeDtypeStruct((dates, rows, samp...]
where the time goes in v3:
time: 50.7 us; the launch traced here: 50 us
  Pallas kernels  43.8 us (86%)
  local copies, waits for them, and re-layouts  5.6 us (11%)
  between operations  0.64 us (1%)
    pallas_call x1, Pallas kernels, on_device(): pl.pallas_call(kernel, out_shape=(jax.ShapeDtypeStruct((dates, rows, samp...  43.8 us
    unnamed x3, local copies, waits for them, and re-layouts  4.28 us
    pallas_call x1, local copies, waits for them, and re-layouts, on_device(): pl.pallas_call(kernel, out_shape=(jax.ShapeDtypeStruct((dates, rows, samp...  1.32 us

profile of v3, /device:TPU:28, one launch (start us, length us, event | category | flops | bytes accessed | tf_op | source)
XLA Modules:
  0.0 50.0 jit_solution(13184982420506911637)
XLA Ops:
  0.6 1.3 %copy.10.at_ref = s32[4,5,20]{2,1,0:T(8,128)} copy(s32[4,5,20]{2,0,1:T(4,128)} %param.9) | data formatting | bytes 3200 | tf_op args[1]
  1.9 1.3 %copy.11.ct_ref = s32[4,5,20]{2,1,0:T(8,128)} copy(s32[4,5,20]{2,0,1:T(4,128)} %param.10) | data formatting | bytes 3200 | tf_op args[2]
  3.2 43.8 %shard_map.95 = (f32[4,5,20]{2,1,0:T(8,128)}, f32[4,2,64,64]{3,2,1,0:T(8,128)}) custom-call(s32[4,5,20]{2,1,0:T(8,128)} %copy.10.at_ref, s32[4,5,20]{2,1,0:T(8,128)} %copy.11.ct_ref, s32[4,5]{1,0:T(4,128)} %pr_ref.1, bf16[4,2,320,1280]{3,2,1,0:T(8,128)(2,1)} %img_ref.1, f32[2,128,128]{2,1,0:T(8,128)} %constant.8.clone.dft_ref, ...), custom_call_target="tpu_custom_call" | custom-call | tf_op jit(solution)/shard_map/pallas_call | solution.py:439
  47.0 1.3 %copy.12 = f32[4,5,20]{2,0,1:T(4,128)} copy(f32[4,5,20]{2,1,0:T(8,128)} %get-tuple-element.2) | data formatting | bytes 3200 | tf_op jit(solution)/shard_map/pallas_call | solution.py:439
  48.3 1.7 %copy.14 = f32[4,2,64,64]{3,2,1,0:T(8,128)} copy(f32[4,2,64,64]{3,2,1,0:T(8,128)} %get-tuple-element.7) | data formatting | bytes 262144

commit v4 on v3

--- a/solution.py
+++ b/solution.py
@@ -14,7 +14,8 @@
 LANES = 128
 PIECE = 16
 AHEAD = 8
-LAG = 3
+LAG = 5
+OPENING = 4
 
 VAR_EPS = 1e-05
 RMS_EPS = 1e-06
@@ -82,7 +83,42 @@
     return x * lax.rsqrt(jnp.maximum(x, TINY))
 
 
-def window_row(p, sizes, at_ref, ct_ref, pr_ref, ref_chunk, blk_ref, rgp_ref, wide, band, prod, pooled, stats, sims, follow):
+def resample(p, d, sizes, at_ref, ct_ref, pr_ref, wide, shifted, devs, stats):
+    dates, lines, strips = sizes
+    lane = lax.broadcasted_iota(jnp.int32, (WIN, LANES), 1)
+    first = lane < WIN
+    near_low = lane < LANES - MARGIN
+    near_high = lane < MARGIN
+    present = pr_ref[d, p]
+    here = pl.ds(pl.multiple_of(p * WIN, WIN), WIN)
+    for m in range(strips):
+        rows = []
+        turns = []
+        for q in (2 * m, 2 * m + 1):
+            start = jnp.where(
+                present != 0, p * WIN + MARGIN + at_ref[p, d, q], lines + 2 * MARGIN
+            )
+            rows.append(pl.ds(start, WIN))
+            turns.append((LANES - ct_ref[p, d, q]) % LANES)
+        part = []
+        for c in range(2):
+            even = wide[d, c, m, rows[0], :]
+            below = wide[d, c, m - 1, rows[0], :] if m > 0 else jnp.zeros_like(even)
+            odd = wide[d, c, m, rows[1], :]
+            above = wide[d, c, m + 1, rows[1], :] if m + 1 < strips else jnp.zeros_like(odd)
+            even = pltpu.roll(jnp.where(near_low, even, below), turns[0], 1)
+            odd = pltpu.roll(jnp.where(near_high, above, odd), turns[1], 1)
+            part.append(jnp.where(first, even, odd))
+            shifted[d, c, m, here, :] = part[c]
+        amp = root(part[0] * part[0] + part[1] * part[1]).reshape(WIN // 8, 8, LANES)
+        mean = jnp.sum(amp, axis=0) * (8.0 / WIN)
+        dev = amp - mean[None]
+        devs[d, m, here, :] = dev.reshape(WIN, LANES)
+        stats[p, 0, m, d] = mean
+        stats[p, 1, m, d] = jnp.sum(dev * dev, axis=0)
+
+
+def window_row(p, sizes, ref_chunk, blk_ref, rgp_ref, shifted, devs, band, prod, pooled, stats, sims, follow):
     dates, lines, strips = sizes
     for m in range(strips):
         cols = slice(m * LANES, (m + 1) * LANES)
@@ -94,41 +130,17 @@
         mean = jnp.sum(amp, axis=0) * (8.0 / WIN)
         dev = amp - mean[None]
         band[2, m] = dev.reshape(WIN, LANES)
-        stats[0, m, dates] = mean
-        stats[1, m, dates] = jnp.sum(dev * dev, axis=0)
+        stats[p, 0, m, dates] = mean
+        stats[p, 1, m, dates] = jnp.sum(dev * dev, axis=0)
 
     def one_date(d, carry):
         follow(d)
-        lane = lax.broadcasted_iota(jnp.int32, (WIN, LANES), 1)
-        first = lane < WIN
-        near_low = lane < LANES - MARGIN
-        near_high = lane < MARGIN
-        present = pr_ref[d, p]
+        here = pl.ds(pl.multiple_of(p * WIN, WIN), WIN)
         for m in range(strips):
-            rows = []
-            turns = []
-            for q in (2 * m, 2 * m + 1):
-                start = jnp.where(
-                    present != 0, p * WIN + MARGIN + at_ref[d, p, q], lines + 2 * MARGIN
-                )
-                rows.append(pl.ds(start, WIN))
-                turns.append((LANES - ct_ref[d, p, q]) % LANES)
-            part = []
-            for c in range(2):
-                even = wide[d, c, m, rows[0], :]
-                below = wide[d, c, m - 1, rows[0], :] if m > 0 else jnp.zeros_like(even)
-                odd = wide[d, c, m, rows[1], :]
-                above = wide[d, c, m + 1, rows[1], :] if m + 1 < strips else jnp.zeros_like(odd)
-                even = pltpu.roll(jnp.where(near_low, even, below), turns[0], 1)
-                odd = pltpu.roll(jnp.where(near_high, above, odd), turns[1], 1)
-                part.append(jnp.where(first, even, odd))
-            sr, si = part
-            amp = root(sr * sr + si * si).reshape(WIN // 8, 8, LANES)
-            mean = jnp.sum(amp, axis=0) * (8.0 / WIN)
-            dev = amp - mean[None]
-            stats[0, m, d] = mean
-            stats[1, m, d] = jnp.sum(dev * dev, axis=0)
-            stats[2, m, d] = jnp.sum(dev * band[2, m].reshape(WIN // 8, 8, LANES), axis=0)
+            sr = shifted[d, 0, m, here, :]
+            si = shifted[d, 1, m, here, :]
+            joint = devs[d, m, here, :] * band[2, m]
+            stats[p, 2, m, d] = jnp.sum(joint.reshape(WIN // 8, 8, LANES), axis=0)
             rr = band[0, m]
             ri = band[1, m]
             for c, value in enumerate((rr * sr + ri * si, ri * sr - rr * si)):
@@ -149,13 +161,13 @@
         return jnp.sum(dot_right(flat, half).reshape(-1, 8, LANES), axis=1, keepdims=True)
 
     count = 8.0 * WIN
-    means = stats[0].reshape(strips * (dates + 1), 8, LANES)
+    means = stats[p, 0].reshape(strips * (dates + 1), 8, LANES)
     away = means - total(means) * (1.0 / count)
-    spread = stats[1].reshape(strips * (dates + 1), 8, LANES)
+    spread = stats[p, 1].reshape(strips * (dates + 1), 8, LANES)
     var = total(spread + (WIN / 8.0) * (away * away)) * (1.0 / (WIN * WIN))
     away = away.reshape(strips, dates + 1, 8, LANES)
     var = var.reshape(strips, dates + 1, 1, LANES)
-    joint = stats[2][:, :dates] + (WIN / 8.0) * (away[:, :dates] * away[:, dates:])
+    joint = stats[p, 2][:, :dates] + (WIN / 8.0) * (away[:, :dates] * away[:, dates:])
     cov = total(joint).reshape(strips, dates, 1, LANES) * (1.0 / (WIN * WIN))
     corr = cov / jnp.sqrt((var[:, dates:] + VAR_EPS) * (var[:, :dates] + VAR_EPS))
     lane = lax.broadcasted_iota(jnp.int32, (dates, 1, LANES), 2)
@@ -217,7 +229,7 @@
 def kernel(
     at_ref, ct_ref, pr_ref, img_ref, dft_ref, blk_ref, azp_ref, rgp_ref,
     sim_ref, out_ref,
-    image, halo, ref, wide, band, prod, pooled, stats, sims,
+    image, halo, ref, wide, shifted, devs, band, prod, pooled, stats, sims,
     image_sem, root_sem, halo_send, halo_recv, ref_send, ref_recv,
 ):
     dates, _, lines, samples = img_ref.shape
@@ -335,26 +347,15 @@
             wide[d, c, m, MARGIN : MARGIN + lines, :] = image[d, c, :, cols].astype(F32)
             wide[d, c, m, 2 * MARGIN + lines : 2 * MARGIN + lines + WIN, :] = jnp.zeros((WIN, LANES), F32)
 
-        @pl.when(i < early)
-        def _():
-            slot(i)
+        @pl.when(i >= 2 * dates - opening)
+        def _():
+            slot(i - (2 * dates - opening))
 
         return carry
 
     early = each + (count - 2) * LAG
+    opening = min(OPENING, 2 * dates)
     lax.fori_loop(0, 2 * dates, widen, 0)
-
-    def catch_up(t, carry):
-        slot(t)
-        return carry
-
-    lax.fori_loop(2 * dates, max(2 * dates, early), catch_up, 0)
-
-    @pl.when(mine == 0)
-    def _():
-        own.wait()
-
-    stats[2] = jnp.zeros(stats.shape[1:], F32)
 
     def fringe(k):
         first = MARGIN + lines if k else 0
@@ -382,12 +383,36 @@
 
             lax.fori_loop(0, 2 * dates, clear, 0)
 
-    def row(s, carry):
-        @pl.when(s == rows - 2)
+    share = -(-(early - opening) // (dates * rows))
+    pace = max(1, dates * rows // max(1, early - opening))
+
+    def shift(i, carry):
+        s = i // dates
+
+        @pl.when((i % pace) == 0)
+        def _():
+            for e in range(share):
+                t = opening + (i // pace) * share + e
+
+                @pl.when(t < early)
+                def _():
+                    slot(t)
+
+        @pl.when(i == (rows - 2) * dates)
         def _():
             for k in range(2):
                 fringe(k)
 
+        resample(row_of(s), i % dates, (dates, lines, strips), at_ref, ct_ref, pr_ref, wide, shifted, devs, stats)
+        return carry
+
+    lax.fori_loop(0, dates * rows, shift, 0)
+
+    @pl.when(mine == 0)
+    def _():
+        own.wait()
+
+    def row(s, carry):
         p = row_of(s)
 
         def ref_chunk(c, cols):
@@ -403,14 +428,14 @@
                     slot(early + s * each + k)
 
         window_row(
-            p, (dates, lines, strips), at_ref, ct_ref, pr_ref, ref_chunk, blk_ref, rgp_ref,
-            wide, band, prod, pooled, stats, sims, follow,
+            p, (dates, lines, strips), ref_chunk, blk_ref, rgp_ref,
+            shifted, devs, band, prod, pooled, stats, sims, follow,
         )
         return carry
 
     lax.fori_loop(0, rows, row, 0)
     for p in range(rows):
-        sim_ref[:, p : p + 1, :] = sims[p][:, :, : sim_ref.shape[2]]
+        sim_ref[p] = sims[p].reshape(dates, LANES)[:, : sim_ref.shape[2]]
     goldstein(dates, out_ref, dft_ref, blk_ref, azp_ref, pooled)
 
     for c in range(2):
@@ -436,10 +461,10 @@
     smem = pl.BlockSpec(memory_space=pltpu.SMEM)
     vmem = pl.BlockSpec(memory_space=pltpu.VMEM)
     dma = pltpu.SemaphoreType.DMA
-    return pl.pallas_call(
+    similarity, filtered = pl.pallas_call(
         kernel,
         out_shape=(
-            jax.ShapeDtypeStruct((dates, rows, samples // WIN), F32),
+            jax.ShapeDtypeStruct((rows, dates, samples // WIN), F32),
             jax.ShapeDtypeStruct((dates, 2, lines // LOOK_AZ, samples // LOOK_RG), F32),
         ),
         in_specs=[smem] * 3 + [pl.BlockSpec(memory_space=pl.ANY)] + [vmem] * 4,
@@ -449,10 +474,12 @@
             pltpu.VMEM((2, dates, 2, MARGIN, samples), BF16),
             pltpu.VMEM((2, lines, samples), BF16),
             pltpu.VMEM((dates, 2, strips, lines + 2 * MARGIN + WIN, LANES), F32),
+            pltpu.VMEM((dates, 2, strips, lines, LANES), F32),
+            pltpu.VMEM((dates, strips, lines, LANES), F32),
             pltpu.VMEM((3, strips, WIN, LANES), F32),
             pltpu.VMEM((dates, 2, WIN, 2 * samples), BF16),
             pltpu.VMEM((dates, 2, lines, samples // LOOK_RG), F32),
-            pltpu.VMEM((3, strips, dates + 1, 8, LANES), F32),
+            pltpu.VMEM((rows, 3, strips, dates + 1, 8, LANES), F32),
             pltpu.VMEM((rows, dates, 1, LANES), F32),
             dma((2 * dates,)),
             dma(()),
@@ -462,9 +489,12 @@
             dma((2, pieces)),
         ],
         compiler_params=pltpu.CompilerParams(
-            vmem_limit_bytes=56 * 1024 * 1024, collective_id=0, has_side_effects=True
+            vmem_limit_bytes=62 * 1024 * 1024, collective_id=0, has_side_effects=True
         ),
-    )(along, cross, present, image, *tables(lines, samples))
+    )(
+        along.transpose(1, 0, 2), cross.transpose(1, 0, 2), present, image, *tables(lines, samples)
+    )
+    return similarity.transpose(1, 0, 2), filtered
 
 
 def solution(mesh):

time: 50.7 us -> 42.5 us (0.84)
  Pallas kernels: 43.8 us -> 38.4 us
  local copies, waits for them, and re-layouts: 5.6 us -> 2.97 us
    pallas_call x1, Pallas kernels: 43.8 us -> 38.4 us  [on_device(): pl.pallas_call(kernel, out_shape=(jax.ShapeDtypeStruct((rows, dates, samp...]
    pallas_call x1 -> x0, local copies, waits for them, and re-layouts: 1.32 us -> none  [on_device(): pl.pallas_call(kernel, out_shape=(jax.ShapeDtypeStruct((dates, rows, samp...]
    unnamed x3 -> x2, local copies, waits for them, and re-layouts: 4.28 us -> 2.97 us
where the time goes in v4:
time: 42.5 us; the launch traced here: 42 us
  Pallas kernels  38.4 us (90%)
  local copies, waits for them, and re-layouts  2.97 us (7%)
  between operations  0.64 us (2%)
    pallas_call x1, Pallas kernels, on_device(): pl.pallas_call(kernel, out_shape=(jax.ShapeDtypeStruct((rows, dates, samp...  38.4 us
    unnamed x2, local copies, waits for them, and re-layouts  2.97 us

profile of v4, /device:TPU:28, one launch (start us, length us, event | category | flops | bytes accessed | tf_op | source)
XLA Modules:
  0.0 42.0 jit_solution(1389258482697709334)
XLA Ops:
  0.6 38.4 %shard_map.95 = (f32[5,4,20]{2,1,0:T(4,128)}, f32[4,2,64,64]{3,2,1,0:T(8,128)}) custom-call(s32[5,4,20]{2,1,0:T(4,128)} %bitcast.3, s32[5,4,20]{2,1,0:T(4,128)} %bitcast.4, s32[4,5]{1,0:T(4,128)} %pr_ref.1, bf16[4,2,320,1280]{3,2,1,0:T(8,128)(2,1)} %img_ref.1, f32[2,128,128]{2,1,0:T(8,128)} %constant.8.clone.dft_ref, ...), custom_call_target="tpu_custom_call" | custom-call | tf_op jit(solution)/shard_map/pallas_call | solution.py:464
  39.0 1.3 %copy.12 = f32[4,5,20]{2,0,1:T(4,128)} copy(f32[4,5,20]{2,0,1:T(4,128)} %bitcast.5) | data formatting | bytes 3200
  40.3 1.7 %copy.13 = f32[4,2,64,64]{3,2,1,0:T(8,128)} copy(f32[4,2,64,64]{3,2,1,0:T(8,128)} %get-tuple-element.9) | data formatting | bytes 262144

commit v5 on v4

--- a/solution.py
+++ b/solution.py
@@ -61,7 +61,9 @@
 
 
 def dot_high(a, b):
-    return jnp.dot(a, b, preferred_element_type=F32, precision=lax.Precision.HIGHEST)
+    a_high, a_low = split(a)
+    b_high, b_low = split(b)
+    return dot(a_high, b_high) + (dot(a_high, b_low) + dot(a_low, b_high))
 
 
 def split(x):
@@ -227,9 +229,9 @@
 
 
 def kernel(
-    at_ref, ct_ref, pr_ref, img_ref, dft_ref, blk_ref, azp_ref, rgp_ref,
-    sim_ref, out_ref,
-    image, halo, ref, wide, shifted, devs, band, prod, pooled, stats, sims,
+    at_ref, ct_ref, pr_ref, img_ref, blk_ref, rgp_ref,
+    sim_ref, pooled,
+    image, halo, ref, wide, shifted, devs, band, prod, stats, sims,
     image_sem, root_sem, halo_send, halo_recv, ref_send, ref_recv,
 ):
     dates, _, lines, samples = img_ref.shape
@@ -436,7 +438,6 @@
     lax.fori_loop(0, rows, row, 0)
     for p in range(rows):
         sim_ref[p] = sims[p].reshape(dates, LANES)[:, : sim_ref.shape[2]]
-    goldstein(dates, out_ref, dft_ref, blk_ref, azp_ref, pooled)
 
     for c in range(2):
         @pl.when(hops[c] < count - 1)
@@ -451,6 +452,11 @@
         @pl.when(sends[k])
         def _():
             edge(k).wait_send()
+
+
+def finish(found_ref, pooled_ref, dft_ref, blk_ref, azp_ref, sim_ref, out_ref):
+    sim_ref[...] = found_ref[...]
+    goldstein(out_ref.shape[0], out_ref, dft_ref, blk_ref, azp_ref, pooled_ref)
 
 
 def on_device(image, along, cross, present):
@@ -461,13 +467,14 @@
     smem = pl.BlockSpec(memory_space=pltpu.SMEM)
     vmem = pl.BlockSpec(memory_space=pltpu.VMEM)
     dma = pltpu.SemaphoreType.DMA
-    similarity, filtered = pl.pallas_call(
+    dft, blocks, az_pool, rg_pool = tables(lines, samples)
+    similarity, pooled = pl.pallas_call(
         kernel,
         out_shape=(
             jax.ShapeDtypeStruct((rows, dates, samples // WIN), F32),
-            jax.ShapeDtypeStruct((dates, 2, lines // LOOK_AZ, samples // LOOK_RG), F32),
+            jax.ShapeDtypeStruct((dates, 2, lines, samples // LOOK_RG), F32),
         ),
-        in_specs=[smem] * 3 + [pl.BlockSpec(memory_space=pl.ANY)] + [vmem] * 4,
+        in_specs=[smem] * 3 + [pl.BlockSpec(memory_space=pl.ANY)] + [vmem] * 2,
         out_specs=(vmem, vmem),
         scratch_shapes=[
             pltpu.VMEM((dates, 2, lines, samples), BF16),
@@ -478,7 +485,6 @@
             pltpu.VMEM((dates, strips, lines, LANES), F32),
             pltpu.VMEM((3, strips, WIN, LANES), F32),
             pltpu.VMEM((dates, 2, WIN, 2 * samples), BF16),
-            pltpu.VMEM((dates, 2, lines, samples // LOOK_RG), F32),
             pltpu.VMEM((rows, 3, strips, dates + 1, 8, LANES), F32),
             pltpu.VMEM((rows, dates, 1, LANES), F32),
             dma((2 * dates,)),
@@ -492,8 +498,17 @@
             vmem_limit_bytes=62 * 1024 * 1024, collective_id=0, has_side_effects=True
         ),
     )(
-        along.transpose(1, 0, 2), cross.transpose(1, 0, 2), present, image, *tables(lines, samples)
+        along.transpose(1, 0, 2), cross.transpose(1, 0, 2), present, image, blocks, rg_pool
     )
+    similarity, filtered = pl.pallas_call(
+        finish,
+        out_shape=(
+            jax.ShapeDtypeStruct(similarity.shape, F32),
+            jax.ShapeDtypeStruct((dates, 2, lines // LOOK_AZ, samples // LOOK_RG), F32),
+        ),
+        in_specs=[vmem] * 5,
+        out_specs=(vmem, vmem),
+    )(similarity, pooled, dft, blocks, az_pool)
     return similarity.transpose(1, 0, 2), filtered
 
 

time: 42.5 us -> 41.4 us (0.974)
  local copies, waits for them, and re-layouts: 2.97 us -> 0 us
  Pallas kernels: 38.4 us -> 40.3 us
    pallas_call x0 -> x1, Pallas kernels: none -> 4.44 us  [on_device(): pl.pallas_call(finish, out_shape=(jax.ShapeDtypeStruct(similarity.shape,...]
    unnamed x2 -> x0, local copies, waits for them, and re-layouts: 2.97 us -> none
    pallas_call x1, Pallas kernels: 38.4 us -> 35.8 us  [on_device(): pl.pallas_call(kernel, out_shape=(jax.ShapeDtypeStruct((rows, dates, samp...]
where the time goes in v5:
time: 41.4 us; the launch traced here: 40.9 us
  Pallas kernels  40.3 us (97%)
  between operations  0.64 us (2%)
    pallas_call x1, Pallas kernels, on_device(): pl.pallas_call(kernel, out_shape=(jax.ShapeDtypeStruct((rows, dates, samp...  35.8 us
    pallas_call x1, Pallas kernels, on_device(): pl.pallas_call(finish, out_shape=(jax.ShapeDtypeStruct(similarity.shape,...  4.44 us

profile of v5, /device:TPU:28, one launch (start us, length us, event | category | flops | bytes accessed | tf_op | source)
XLA Modules:
  0.0 40.9 jit_solution(12063138825304572666)
XLA Ops:
  0.6 35.8 %shard_map.95 = (f32[5,4,20]{2,1,0:T(4,128)}, f32[4,2,320,64]{3,2,1,0:T(8,128)}) custom-call(s32[5,4,20]{2,1,0:T(4,128)} %bitcast.3, s32[5,4,20]{2,1,0:T(4,128)} %bitcast.4, s32[4,5]{1,0:T(4,128)} %pr_ref.1, bf16[4,2,320,1280]{3,2,1,0:T(8,128)(2,1)} %img_ref.1, bf16[3,128,128]{2,1,0:T(8,128)(2,1)} %constant.9.clone.blk_ref, ...), custom_call_target="tpu_custom_call" | custom-call | tf_op jit(solution)/shard_map/pallas_call | solution.py:471
  36.5 4.4 %shard_map.96 = (f32[5,4,20]{2,1,0:T(4,128)}, f32[4,2,64,64]{3,2,1,0:T(8,128)}) custom-call(f32[5,4,20]{2,1,0:T(4,128)} %get-tuple-element.6.found_ref, f32[4,2,320,64]{3,2,1,0:T(8,128)} %get-tuple-element.7.pooled_ref, f32[2,128,128]{2,1,0:T(8,128)} %constant.8.clone.dft_ref, bf16[3,128,128]{2,1,0:T(8,128)(2,1)} %constant.9.clone.blk_ref, ...), custom_call_target="tpu_custom_call" | custom-call | tf_op jit(solution)/shard_map/pallas_call | solution.py:503
